TPU v7x, 32 devices: a whole 2x2x4 slice. The times are simulated.
32 devices in a mesh: crop: 8 (over z, y), head: 4 (over x, core).
Axes of the slice: x: 2, y: 2, z: 4, core: 2. Of those that a mesh axis runs over, the one named last changes fastest.
Arguments:
- tokens: bfloat16 [16384, 768], P(('crop', 'head')), may hold values from -6 to 6
- mix_weight: float32 [16384], P(('crop', 'head')), may hold values from 0.5 to 0.9
- partner_row: int32 [16384], P(('crop', 'head')), may hold values from 0 to 511
- crop_lengths: int32 [8, 2], P('crop'), may hold values from 416 to 1632, as said below
- ln1_gain: bfloat16 [768], replicated, may hold values from 0.5 to 1.5
- ln1_bias: bfloat16 [768], replicated, may hold values from -1.5 to 1.5
- w_qkv: bfloat16 [768, 2304], replicated, may hold values from -0.21875 to 0.21875
- b_query: bfloat16 [768], replicated, may hold values from -1.5 to 1.5
- b_value: bfloat16 [768], replicated, may hold values from -1.5 to 1.5
- w_out: bfloat16 [768, 768], replicated, may hold values from -2.5 to 2.5
- b_out: bfloat16 [768], replicated, may hold values from -1.5 to 1.5
- ln2_gain: bfloat16 [768], replicated, may hold values from 0.5 to 1.5
- ln2_bias: bfloat16 [768], replicated, may hold values from -1.5 to 1.5
- w_fc1: bfloat16 [768, 3072], replicated, may hold values from -0.21875 to 0.21875
- b_fc1: bfloat16 [3072], replicated, may hold values from -1.5 to 1.5
- w_fc2: bfloat16 [3072, 768], replicated, may hold values from -0.109375 to 0.109375
- b_fc2: bfloat16 [768], replicated, may hold values from -1.5 to 1.5
- cotangent: bfloat16 [16384, 768], P(('crop', 'head')), may hold values from -6 to 6
Outputs:
- layer_out: bfloat16 [16384, 768], P(('crop', 'head'))
- input_grad: bfloat16 [16384, 768], P(('crop', 'head'))
- grad_ln1_gain: float32 [768], P('crop')
- grad_ln1_bias: float32 [768], P('crop')
- grad_w_qkv: float32 [768, 2304], P('crop')
- grad_b_query: float32 [768], P('crop')
- grad_b_value: float32 [768], P('crop')
- grad_w_out: float32 [768, 768], P('crop')
- grad_b_out: float32 [768], P('crop')
- grad_ln2_gain: float32 [768], P('crop')
- grad_ln2_bias: float32 [768], P('crop')
- grad_w_fc1: float32 [768, 3072], P('crop')
- grad_b_fc1: float32 [3072], P('crop')
- grad_w_fc2: float32 [3072, 768], P('crop')
- grad_b_fc2: float32 [768], P('crop')
Inputs may be any that keep to these rules, and one draw needn't show every extreme that they name: `crop_lengths`: each row holds the 2 crop lengths of one group; they sum to 2048; in every group one crop starts within the first 512 rows of the group and ends within its last 512 rows.
All inputs are finite; a program needn't handle non-finite values.
Results may differ from a plain program's by a relative error of at most 0.014.
Values may be sent and summed in bfloat16 or wider, within the bound.
A program may use at most 192 MiB of HBM per device.

v0:
```python
import functools
import itertools

import jax
import jax.numpy as jnp
from jax import lax
from jax.experimental import pallas as pl
from jax.experimental.pallas import tpu as pltpu
from jax.sharding import PartitionSpec as P

HEADS = 12
HEAD_DIM = 64
EPS = 1e-06
NEG = -1e30
KEYS = 64
LANES = 256
FC_TILE = 768
MESH = pl.DeviceIdType.MESH
F32 = jnp.float32
BF16 = jnp.bfloat16
MiB = 1 << 20


def dot(left, right):
    return jnp.dot(left, right, preferred_element_type=F32)


def dot_nt(left, right):
    return lax.dot_general(left, right, (((1,), (1,)), ((), ())), preferred_element_type=F32)


def dot_tn(left, right):
    return lax.dot_general(left, right, (((0,), (0,)), ((), ())), preferred_element_type=F32)


def as_line(ref):
    return ref[...].reshape(1, ref.shape[0])


def as_column(row):
    return jnp.transpose(jnp.broadcast_to(row, (8, row.shape[1])))[:, 0:1]


def as_row(column):
    return jnp.transpose(jnp.broadcast_to(column, (column.shape[0], 128)))[0:8]


def halves_to_lanes(block):
    half = block.shape[0] // 2
    return jnp.concatenate([block[:half], block[half:]], axis=1)


def lanes_to_halves(block):
    return jnp.concatenate([block[:, :HEAD_DIM], block[:, HEAD_DIM:]], axis=0)


def greet(peers):
    barrier = pltpu.get_barrier_semaphore()
    for peer in peers:
        pl.semaphore_signal(barrier, inc=1, device_id=peer, device_id_type=MESH)
    pl.semaphore_wait(barrier, len(peers))


def sorted_blocks(first_case, parts):
    end = lax.select(first_case, parts[0], parts[3])
    full = lax.select(first_case, parts[3], parts[0])
    q = end.shape[0] // 4
    near = lax.select(first_case, end[:q], end[3 * q :])
    either = lax.select(first_case, end[3 * q :], end[:q])
    return [near, end[q : 3 * q], either, full, parts[1], parts[2]]


def unsorted_blocks(first_case, block):
    n = block.shape[0] // 4
    q = n // 4
    low, mid, top = block[:q], block[q : 3 * q], block[3 * q : n]
    head = lax.select(first_case, low, top)
    tail = lax.select(first_case, top, low)
    end = jnp.concatenate([head, mid, tail], axis=0)
    full = block[n : 2 * n]
    return [
        lax.select(first_case, end, full),
        block[2 * n : 3 * n],
        block[3 * n :],
        lax.select(first_case, full, end),
    ]


def either_in_long(first_case, bound, shape, axis, group):
    place = lax.broadcasted_iota(jnp.int32, shape, axis)
    row = place + jnp.where(first_case, group // 4 - 128, group - group // 4)
    past = row >= bound
    return jnp.where(first_case, past.astype(F32), 1.0 - past.astype(F32))


def front_kernel(
    n_crop,
    n_head,
    tokens, mixw_r, prow_r, crop, gain_r, bias_r, bq_r, bv_r, wqkv, cot, w2_h,
    mixed_o, normed_o, grp_o, att_o, own_o, lse_o, gw_o, cott_o, gsum_o,
    prt, mixed_s, normed_s, msg, grp, q_s, k_s, v_s, o_s, qt_s, vt_s, ot_s, s_s, p_s, tot_s, own_s, att_r, w2, gw_s, cott_s,
    prt_sem, qkv_send, qkv_recv, att_send, att_recv, own_sem, out_sem, w2_sem, gw_sem,
):
    rows, width = tokens.shape
    group = rows * n_head
    local = HEADS // n_head
    c, h = lax.axis_index("crop"), lax.axis_index("head")
    far = lax.rem(c + n_crop // 2, n_crop)
    others = [lax.rem(h + o, n_head) for o in range(1, n_head)]
    greet([(far, h)] + [(c, other) for other in others])

    partner_copy = pltpu.make_async_remote_copy(
        src_ref=tokens, dst_ref=prt, send_sem=prt_sem.at[0], recv_sem=prt_sem.at[1], device_id=(far, h), device_id_type=MESH
    )
    partner_copy.start()
    mixw, prow = as_line(mixw_r), as_line(prow_r)
    gain, bias, query_bias, value_bias = [as_line(r).astype(F32) for r in (gain_r, bias_r, bq_r, bv_r)]
    share = as_column(mixw)
    chosen = lax.broadcasted_iota(jnp.int32, (rows, rows), 0) == prow
    chosen = chosen.astype(F32).astype(BF16)
    tiles = w2.shape[0]
    w2_copies = [
        pltpu.make_async_copy(w2_h.at[t * w2.shape[1] : (t + 1) * w2.shape[1]], w2.at[t], w2_sem.at[t]) for t in range(tiles)
    ]
    for copy in w2_copies:
        copy.start()
    gsum_o[...] = jnp.broadcast_to(jnp.sum(cot[...].astype(F32), axis=0, keepdims=True), gsum_o.shape)
    cott_s[...] = jnp.transpose(cot[...])
    gw_copies = [pltpu.make_async_copy(cott_s, cott_o, gw_sem.at[tiles])]
    gw_copies[0].start()
    for t in range(tiles):
        w2_copies[t].wait()
        gw_s[t] = dot_nt(cot[...], w2[t])
        gw_copies.append(pltpu.make_async_copy(gw_s.at[t], gw_o.at[t], gw_sem.at[t]))
        gw_copies[-1].start()
    partner_copy.wait()
    step = 128
    for r in range(0, rows, step):
        part = slice(r, r + step)
        gathered = dot_tn(chosen[:, part], prt[...])
        mix = share[part] * tokens[part].astype(F32) + (1.0 - share[part]) * gathered
        mixed_s[part] = mix
        mean = jnp.mean(mix, axis=1, keepdims=True)
        centered = mix - mean
        variance = jnp.mean(centered * centered, axis=1, keepdims=True)
        normed = centered * lax.rsqrt(variance + EPS) * gain + bias
        normed_s[part] = normed.astype(BF16)
    outs = [
        pltpu.make_async_copy(mixed_s, mixed_o, out_sem.at[0]),
        pltpu.make_async_copy(normed_s, normed_o, out_sem.at[1]),
    ]
    for out in outs:
        out.start()

    qkv_copies = []
    for j in range(local):
        for d in range(n_head):
            i = d * local + j
            odd = i % 2
            base = 3 * HEAD_DIM * i - HEAD_DIM * odd
            res = dot(normed_s[...], wqkv[:, base : base + 4 * HEAD_DIM])
            res = res[:, HEAD_DIM * odd : HEAD_DIM * odd + 3 * HEAD_DIM]
            bq = query_bias[:, HEAD_DIM * i : HEAD_DIM * (i + 1)]
            bv = value_bias[:, HEAD_DIM * i : HEAD_DIM * (i + 1)]
            res = res + jnp.concatenate([bq, jnp.zeros_like(bq), bv], axis=1)
            msg[i, 0:rows] = res[:, : 2 * HEAD_DIM].astype(BF16)
            msg[i, rows : rows + rows // 2] = halves_to_lanes(res[:, 2 * HEAD_DIM :]).astype(BF16)
        batch = [pltpu.make_async_copy(msg.at[h * local + j], grp.at[j, h], own_sem.at[j])]
        for o, other in enumerate(others):
            batch.append(
                pltpu.make_async_remote_copy(
                    src_ref=msg.at[other * local + j],
                    dst_ref=grp.at[j, h],
                    send_sem=qkv_send.at[j, o],
                    recv_sem=qkv_recv.at[j, o],
                    device_id=(c, other),
                    device_id_type=MESH,
                )
            )
        qkv_copies.append(batch)
        if j == 0:
            for copy in batch:
                copy.start()

    bound = crop[0, 0]
    first_case = bound < group // 2
    quarter = rows // 4
    short, long0 = 3 * quarter, 4 * quarter
    in_col = either_in_long(first_case, bound, (quarter, 1), 0, group) > 0.5
    in_row = either_in_long(first_case, bound, (1, quarter), 1, group) > 0.5
    col_long, col_short = jnp.where(in_col, 0.0, NEG), jnp.where(in_col, NEG, 0.0)
    row_long, row_short = jnp.where(in_row, 0.0, NEG), jnp.where(in_row, NEG, 0.0)
    att_copies = []
    for j in range(local):
        for copy in qkv_copies[j]:
            copy.wait()
        if j + 1 < local:
            for copy in qkv_copies[j + 1]:
                copy.start()
        qk = sorted_blocks(first_case, [grp[j, s, 0:rows] for s in range(n_head)])
        vv = sorted_blocks(first_case, [lanes_to_halves(grp[j, s, rows : rows + rows // 2]) for s in range(n_head)])
        at = 0
        for a, b in zip(qk, vv):
            n = a.shape[0]
            q_s[at : at + n] = a[:, :HEAD_DIM] * BF16(HEAD_DIM**-0.5)
            k_s[at : at + n] = a[:, HEAD_DIM:]
            v_s[at : at + n] = b
            at += n

        qt_s[...] = jnp.transpose(q_s[...])
        vt_s[...] = jnp.transpose(v_s[...])

        def area(slot, q0, count, k0, k1, masks):
            lanes, number = slice(q0, q0 + count), k1 - k0
            s_s[slot, :number, :count] = dot(k_s[k0:k1], qt_s[:, lanes])
            for k, mask in masks.items():
                s_s[slot, k - k0 : k - k0 + quarter, :count] += mask
            for at in range(0, count, LANES):
                wide = min(LANES, count - at)
                here = slice(at, at + wide)
                top = jnp.full((8, wide), NEG, F32)
                for k in range(0, number, KEYS):
                    top = jnp.maximum(top, jnp.max(s_s[slot, k : k + KEYS, here].reshape(KEYS // 8, 8, wide), axis=0))
                top = jnp.max(top, axis=0, keepdims=True)
                total = jnp.zeros((8, wide), F32)
                for k in range(0, number, KEYS):
                    p = jnp.exp(s_s[slot, k : k + KEYS, here] - top)
                    total = total + jnp.sum(p.reshape(KEYS // 8, 8, wide), axis=0)
                    p_s[slot, k : k + KEYS, here] = p.astype(BF16)
                total = jnp.sum(total, axis=0, keepdims=True)
                tot_s[slot : slot + 1, here] = 1.0 / total
                lse_o[j : j + 1, q0 + at : q0 + at + wide] = top + jnp.log(total)
            out = dot(vt_s[:, k0:k1], p_s[slot, :number, :count])
            ot_s[:, lanes] = out * tot_s[slot : slot + 1, :count]

        area(0, 0, short, 0, long0, {short: col_short})
        either = {k: row_short for k in range(0, short, quarter)}
        either[short] = jnp.where(in_row, col_long, col_short)
        either.update({k: row_long for k in range(long0, group, quarter)})
        area(1, short, quarter, 0, group, either)
        for t in range(n_head - 1):
            area(t % 2, long0 + t * rows, rows, short, group, {short: col_long})
        o_s[...] = jnp.transpose(ot_s[...]).astype(BF16)

        for s, block in enumerate(unsorted_blocks(first_case, o_s[...])):
            own_s[j, s] = halves_to_lanes(block)
        batch = [pltpu.make_async_copy(own_s.at[j, h], att_r.at[h * local + j], own_sem.at[j])]
        for o, other in enumerate(others):
            batch.append(
                pltpu.make_async_remote_copy(
                    src_ref=own_s.at[j, other],
                    dst_ref=att_r.at[h * local + j],
                    send_sem=att_send.at[j, o],
                    recv_sem=att_recv.at[j, o],
                    device_id=(c, other),
                    device_id_type=MESH,
                )
            )
        for copy in batch:
            copy.start()
        att_copies.append(batch)
    late = [pltpu.make_async_copy(grp, grp_o, out_sem.at[2]), pltpu.make_async_copy(own_s, own_o, out_sem.at[3])]
    for out in late:
        out.start()
    outs += late
    for batch in att_copies:
        for copy in batch:
            copy.wait()
    for p in range(HEADS // 2):
        even, odd = att_r[2 * p], att_r[2 * p + 1]
        top = jnp.concatenate([even[:, :HEAD_DIM], odd[:, :HEAD_DIM]], axis=1)
        low = jnp.concatenate([even[:, HEAD_DIM:], odd[:, HEAD_DIM:]], axis=1)
        att_o[:, 128 * p : 128 * (p + 1)] = jnp.concatenate([top, low], axis=0)
    for out in outs + gw_copies:
        out.wait()


def front(n_crop, n_head, tokens, mixw, prow, crop, small, wqkv, cot, w2):
    rows, width = tokens.shape
    group, local = rows * n_head, HEADS // n_head
    dma = pltpu.SemaphoreType.DMA
    vmem = pl.BlockSpec(memory_space=pltpu.VMEM)
    hbm = pl.BlockSpec(memory_space=pl.ANY)
    block = rows + rows // 2
    shape = jax.ShapeDtypeStruct
    return pl.pallas_call(
        functools.partial(front_kernel, n_crop, n_head),
        out_shape=(
            shape((rows, width), F32),
            shape((rows, width), BF16),
            shape((local, n_head, block, 128), BF16),
            shape((rows, width), BF16),
            shape((local, n_head, rows // 2, 128), BF16),
            shape((8, group), F32),
            shape((w2.shape[0] // FC_TILE, rows, FC_TILE), F32),
            shape((width, rows), BF16),
            shape((8, width), F32),
        ),
        in_specs=[vmem, vmem, vmem, pl.BlockSpec(memory_space=pltpu.SMEM), vmem, vmem, vmem, vmem, vmem, vmem, hbm],
        out_specs=(hbm, hbm, hbm, vmem, hbm, vmem, hbm, hbm, vmem),
        scratch_shapes=[
            pltpu.VMEM((rows, width), BF16),
            pltpu.VMEM((rows, width), F32),
            pltpu.VMEM((rows, width), BF16),
            pltpu.VMEM((HEADS, block, 128), BF16),
            pltpu.VMEM((local, n_head, block, 128), BF16),
            pltpu.VMEM((group, HEAD_DIM), BF16),
            pltpu.VMEM((group, HEAD_DIM), BF16),
            pltpu.VMEM((group, HEAD_DIM), BF16),
            pltpu.VMEM((group, HEAD_DIM), BF16),
            pltpu.VMEM((HEAD_DIM, group), BF16),
            pltpu.VMEM((HEAD_DIM, group), BF16),
            pltpu.VMEM((HEAD_DIM, group), F32),
            pltpu.VMEM((2, group, rows), F32),
            pltpu.VMEM((2, group, rows), BF16),
            pltpu.VMEM((8, rows), F32),
            pltpu.VMEM((local, n_head, rows // 2, 128), BF16),
            pltpu.VMEM((HEADS, rows // 2, 128), BF16),
            pltpu.VMEM((w2.shape[0] // FC_TILE, FC_TILE, width), BF16),
            pltpu.VMEM((w2.shape[0] // FC_TILE, rows, FC_TILE), F32),
            pltpu.VMEM((width, rows), BF16),
            dma((2,)),
            dma((local, n_head - 1)),
            dma((local, n_head - 1)),
            dma((local, n_head - 1)),
            dma((local, n_head - 1)),
            dma((local,)),
            dma((4,)),
            dma((4,)),
            dma((5,)),
        ],
        compiler_params=pltpu.CompilerParams(collective_id=1, has_side_effects=True, vmem_limit_bytes=60 * MiB),
        cost_estimate=pl.CostEstimate(flops=10**10, bytes_accessed=2 * 10**7, transcendentals=10**7),
        name="front",
    )(tokens, mixw, prow, crop, *small, wqkv, cot, w2)


GELU_POLY = (0.254829592, -0.284496736, 1.421413741, -1.453152027, 1.061405429)
PIECE = 384


def gelu_and_slope(pre):
    bell = jnp.exp(-0.5 * pre * pre)
    t = 1.0 / (1.0 + (0.3275911 * 0.7071067811865476) * jnp.abs(pre))
    poly = GELU_POLY[4]
    for coefficient in GELU_POLY[3::-1]:
        poly = poly * t + coefficient
    tail = 0.5 * poly * t * bell
    phi = jnp.where(pre >= 0.0, 1.0 - tail, tail)
    return pre * phi, phi + pre * bell * 0.3989422804014327


def put_blocks(ref, lead, value):
    if len(ref.shape) == len(lead) + 5:
        rows = value.shape[0] // 8
        for c in range(8):
            ref[(*lead, c % 2, c // 2 % 2, c // 4)] = value[c * rows : (c + 1) * rows].astype(BF16)
    else:
        ref[lead] = value.astype(BF16)


def middle_kernel(
    cut,
    att, mixed, cot, cott, gsum, bout_r, gain_r, bias_r, bfc2_r, bfc1_r, wout_h, w1_h, w2_h, gw_h,
    layer_o, attg_o, mg_o, jfc_o, gout_o, sm_o,
    wout, w1, w2, mid_s, n2_s, n2t_s, out_s, dn_s, pre_s, gw_s, act_s, pg_s, proj_s, jfc,
    w_sem, j_sem,
):
    rows, width = cot.shape
    tiles = w1_h.shape[1] // FC_TILE
    wout_copy = pltpu.make_async_copy(wout_h, wout, w_sem.at[0, 0])
    wout_copy.start()
    w_copies = []
    for t in range(tiles):
        at = slice(t * FC_TILE, (t + 1) * FC_TILE)
        pair = (
            pltpu.make_async_copy(w1_h.at[:, at], w1.at[t], w_sem.at[1, t]),
            pltpu.make_async_copy(gw_h.at[t], gw_s.at[t], w_sem.at[3, t]),
            pltpu.make_async_copy(w2_h.at[at], w2.at[t], w_sem.at[2, t]),
        )
        for copy in pair:
            copy.start()
        w_copies.append(pair)
    sm_o[...] = jnp.zeros_like(sm_o)
    bout, gain, bias, bfc2, bfc1 = [as_line(r).astype(F32) for r in (bout_r, gain_r, bias_r, bfc2_r, bfc1_r)]
    wout_copy.wait()
    step = 128
    mid_s[...] = mixed[...] + dot(att[...], wout[...]) + bout

    def norm2(part):
        mid = mid_s[part]
        mean = jnp.mean(mid, axis=1, keepdims=True)
        centered = mid - mean
        rstd = lax.rsqrt(jnp.mean(centered * centered, axis=1, keepdims=True) + EPS)
        return mid, centered * rstd, rstd

    for r in range(0, rows, step):
        part = slice(r, r + step)
        mid, unit, _ = norm2(part)
        n2_s[part] = (unit * gain + bias).astype(BF16)
        out_s[part] = mid + bfc2
        dn_s[part] = jnp.zeros((step, width), F32)
    sm_o[7:8, :] = gsum[0:1, :]
    n2t_s[...] = jnp.transpose(n2_s[...])

    def first_products(t):
        for copy in w_copies[t]:
            copy.wait()
        pre_s[t % 2] = dot(n2_s[...], w1[t]) + bfc1[:, t * FC_TILE : (t + 1) * FC_TILE]

    j_copies = []
    first_products(0)
    for t in range(tiles):
        now, core, x = t % 2, t % 2, t // 2
        if t + 1 < tiles:
            first_products(t + 1)
        sums = jnp.zeros((1, FC_TILE), F32)
        for r in range(0, rows, 32):
            part = slice(r, r + 32)
            act, slope = gelu_and_slope(pre_s[now, part])
            act_s[now, part] = act.astype(BF16)
            pg = (gw_s[t, part] * slope).astype(BF16)
            pg_s[now, part] = pg
            sums = sums + jnp.sum(pg.astype(F32), axis=0, keepdims=True)
        sm_o[8 + t : 9 + t, :] = sums
        out_s[...] += dot(act_s[now], w2[t])
        dn_s[...] += dot_nt(pg_s[now], w1[t])
        g1 = dot(n2t_s[...], pg_s[now])
        for half in range(2):
            put_blocks(jfc, (half, core, x), g1[:, PIECE * half : PIECE * (half + 1)])
        g2 = dot(cott[...], act_s[now])
        places = [(0, core, x), (1, core, x)]
        if cut:
            for b in range(8):
                for s in range(2):
                    piece = g2[96 * b : 96 * (b + 1), PIECE * s : PIECE * (s + 1)].astype(BF16)
                    jfc[2 + b % 2, b // 2 % 2, b // 4, s, core, x] = piece
            places.append((slice(2, 4), slice(0, 2), slice(0, 2), slice(0, 2), core, x))
        else:
            for half in range(2):
                jfc[2 + half, core, x] = g2[:, PIECE * half : PIECE * (half + 1)].astype(BF16)
            places += [(2, core, x), (3, core, x)]
        for n, place in enumerate(places):
            j_copies.append(pltpu.make_async_copy(jfc.at[place], jfc_o.at[place], j_sem.at[t, n]))
            j_copies[-1].start()

    sums = [jnp.zeros((1, width), F32)] * 3
    for r in range(0, rows, step):
        part = slice(r, r + step)
        layer_o[part] = out_s[part].astype(BF16)
        _, unit, rstd = norm2(part)
        dn = dn_s[part]
        e = dn * gain
        inner = e - jnp.mean(e, axis=1, keepdims=True) - unit * jnp.mean(e * unit, axis=1, keepdims=True)
        mg = cot[part].astype(F32) + rstd * inner
        mg_o[part] = mg
        proj = mg.astype(BF16)
        proj_s[part] = proj
        for k, term in enumerate((proj.astype(F32), dn * unit, dn)):
            sums[k] = sums[k] + jnp.sum(term, axis=0, keepdims=True)
    for k in range(3):
        sm_o[4 + k : 5 + k, :] = sums[k]
    attg = dot_nt(proj_s[...], wout[...])
    for i in range(HEADS):
        attg_o[i] = halves_to_lanes(attg[:, HEAD_DIM * i : HEAD_DIM * (i + 1)]).astype(BF16)
    gout = dot_tn(att[...], proj_s[...])
    for k in range(2):
        put_blocks(gout_o, (k,), gout[:, PIECE * k : PIECE * (k + 1)])
    for copy in j_copies:
        copy.wait()


def middle(cut, att, mixed, cot, cott, gsum, small, wout, w1, w2, gw):
    rows, width = cot.shape
    vmem = pl.BlockSpec(memory_space=pltpu.VMEM)
    hbm = pl.BlockSpec(memory_space=pl.ANY)
    dma = pltpu.SemaphoreType.DMA
    shape = jax.ShapeDtypeStruct
    ff = w1.shape[1]
    jfc_dims = (4, 2, 2, 2, 2, 2, 96, PIECE) if cut else (4, 2, 2, width, PIECE)
    gout_dims = (2, 2, 2, 2, 96, PIECE) if cut else (2, width, PIECE)
    full = lambda kind: pltpu.VMEM((rows, width), kind)
    tile = lambda kind: pltpu.VMEM((2, rows, FC_TILE), kind)
    return pl.pallas_call(
        functools.partial(middle_kernel, cut),
        out_shape=(
            shape((rows, width), BF16),
            shape((HEADS, rows // 2, 128), BF16),
            shape((rows, width), F32),
            shape(jfc_dims, BF16),
            shape(gout_dims, BF16),
            shape((16, width), F32),
        ),
        in_specs=[vmem] * 10 + [hbm] * 4,
        out_specs=(vmem, vmem, vmem, hbm, vmem, vmem),
        scratch_shapes=[
            pltpu.VMEM((width, width), BF16),
            pltpu.VMEM((ff // FC_TILE, width, FC_TILE), BF16),
            pltpu.VMEM((ff // FC_TILE, FC_TILE, width), BF16),
            full(F32), full(BF16),
            pltpu.VMEM((width, rows), BF16),
            full(F32), full(F32), tile(F32), pltpu.VMEM(gw.shape, F32), tile(BF16), tile(BF16), full(BF16),
            pltpu.VMEM(jfc_dims, BF16),
            dma((4, 4)), dma((4, 4)),
        ],
        compiler_params=pltpu.CompilerParams(vmem_limit_bytes=60 * MiB),
        cost_estimate=pl.CostEstimate(flops=2 * 8 * 10**9, bytes_accessed=3 * 10**7, transcendentals=4 * 10**6),
        name="middle",
    )(att, mixed, cot, cott, gsum, *small, wout, w1, w2, gw)


class Reduction:
    AXES = ("x", "y", "lo", "hi")

    def __init__(self, acc, received, fin, send_sem, recv_sem, bits, peers, others, order):
        self.acc, self.received, self.fin = acc, received, fin
        self.send_sem, self.recv_sem = send_sem, recv_sem
        self.bits, self.peers, self.others, self.order = bits, peers, others, order

    def remote(self, k, src, dst, axis, peer=None):
        return pltpu.make_async_remote_copy(
            src_ref=src, dst_ref=dst, send_sem=self.send_sem.at[k], recv_sem=self.recv_sem.at[k],
            device_id=peer or self.peers[axis], device_id_type=MESH,
        )

    def add(self, into, received, lead, free):
        for place in itertools.product((0, 1), repeat=len(free)):
            index = list(lead)
            for axis, p in zip(free, place):
                index[self.AXES.index(axis)] = p
            index = tuple(index)
            into[index] = into[index] + received[place]

    def steps(self, source, core_half):
        copy = self.remote(0, source, self.received[0], "core")
        copy.start()
        if core_half is not None:
            core_half.start()
        yield
        copy.wait()
        if core_half is not None:
            core_half.wait()
        self.add(self.acc, self.received[0], [None] * 4, list(self.AXES))
        lead = [slice(None)] * 4
        free = list(self.AXES)
        for k, axis in enumerate(self.order):
            at = self.AXES.index(axis)
            lead[at] = 1 - self.bits[axis]
            copy = self.remote(1 + k, self.acc.at[tuple(lead)], self.received[1 + k], axis)
            copy.start()
            lead[at] = self.bits[axis]
            free.remove(axis)
            yield
            copy.wait()
            self.add(self.acc, self.received[1 + k], lead, free)
        bc, bx = self.bits["core"], self.bits["x"]
        mine = pltpu.make_async_copy(self.acc.at[tuple(lead)], self.fin.at[bc, bx], self.send_sem.at[8])
        mine.start()
        mine.wait()
        copies = [
            self.remote(5 + n, self.fin.at[bc, bx], self.fin.at[bc, bx], None, other) for n, other in enumerate(self.others)
        ]
        for copy in copies:
            copy.start()
        yield
        for copy in copies:
            copy.wait()


def tick(*jobs):
    for job in jobs:
        next(job, None)


def back_kernel(
    n_crop, n_head, cut,
    attg, grp_h, own, lse, jfc_h, gout, wqkv_h, normed_h, mixed_h, mg_h, mixw_r, prow_r, crop, gain_r, sm_in,
    *rest,
):
    (
        grad_o, fin_o, sm_o,
        grp, wqkv, normt, mixed, mg_s, dor, k_s, v_s, kt_s, qt_s, dot_s, dqt_s, s_s, dp_s, pds_s, dzq_s, dkv_s, dq_s, di_s, msg, ret, dn_s, sent_s, back_s,
        ja, jb, load_sem, do_send, do_recv, dq_send, dq_recv, own_sem, far_sem,
        *reduce_refs,
    ) = rest
    rows, width = mixed.shape
    group = rows * n_head
    local = HEADS // n_head
    c, h = lax.axis_index("crop"), lax.axis_index("head")
    far = lax.rem(c + n_crop // 2, n_crop)
    others = [lax.rem(h + o, n_head) for o in range(1, n_head)]
    peers = [(far, h)] + [(c, other) for other in others]
    if cut:
        bits = {"core": lax.rem(h, 2), "x": lax.div(h, 2), "y": lax.rem(c, 2), "lo": lax.rem(lax.div(c, 2), 2), "hi": lax.div(c, 4)}
        near = {
            "core": (c, h + 1 - 2 * bits["core"]),
            "x": (c, h + 2 - 4 * bits["x"]),
            "y": (c + 1 - 2 * bits["y"], h),
            "lo": (c + 2 - 4 * bits["lo"], h),
            "hi": (far, h),
        }
        peers += [near["y"], near["lo"]]
    greet(peers)

    def spread(j, source, target, send_sem, recv_sem):
        copies = [pltpu.make_async_copy(source(h), target(h), own_sem.at[j])]
        for o, other in enumerate(others):
            copies.append(
                pltpu.make_async_remote_copy(
                    src_ref=source(other), dst_ref=target(h), send_sem=send_sem.at[j, o], recv_sem=recv_sem.at[j, o],
                    device_id=(c, other), device_id_type=MESH,
                )
            )
        return copies

    def start(copies):
        for copy in copies:
            copy.start()

    do_copies = [
        spread(j, lambda d, j=j: attg.at[d * local + j], lambda s, j=j: dor.at[j, s], do_send, do_recv) for j in range(local)
    ]
    start(do_copies[0])
    loads = [
        pltpu.make_async_copy(a, b, load_sem.at[k])
        for k, (a, b) in enumerate([(grp_h, grp), (normed_h, sent_s), (wqkv_h, wqkv), (mixed_h, mixed), (mg_h, mg_s)])
    ]
    loads += [pltpu.make_async_copy(gout.at[k], ja.at[k, 0], load_sem.at[5 + k]) for k in range(2)]
    for load in loads:
        load.start()
    jobs, plan = [], {}
    if cut:
        send_sem, recv_sem, half_sem, sm_send, sm_recv, sm_r, acc_s, *received = reduce_refs
        orders = [
            ("y", "hi", "lo", "x"), ("lo", "y", "hi", "x"), ("y", "lo", "hi", "x"), ("lo", "y", "hi", "x"),
            ("lo", "x", "y", "hi"), ("y", "x", "lo", "hi"),
        ]
        for k in range(6):
            acc = acc_s.at[k] if k < 4 else (ja, jb)[k - 4].at[bits["core"]]
            red = Reduction(acc, [r.at[k] for r in received], fin_o.at[k], send_sem.at[k], recv_sem.at[k], bits, near, peers[1:n_head], orders[k])
            if k < 4:
                keep = pltpu.make_async_copy(jfc_h.at[k, bits["core"]], acc, half_sem.at[k])
                jobs.append(red.steps(jfc_h.at[k, 1 - bits["core"]], keep))
            else:
                jobs.append(red.steps((ja, jb)[k - 4].at[1 - bits["core"]], None))
        fc1, fc2, fc3, fc4, joba, jobb = jobs
        plan = {
            (0, "first"): (fc1, fc2),
            (0, 2): (fc1, fc2, fc3, fc4),
            (1, 2): (fc1, fc2, fc3, fc4),
            (1, "end"): (joba,),
            (2, 2): (fc1, fc2, fc4),
            (2, 5): (fc3, joba, fc1),
            (2, "end"): (fc2, fc4),
            "last": (jobb, fc3, fc1, fc4, fc2),
        }

    bound = crop[0, 0]
    first_case = bound < group // 2
    quarter = rows // 4
    short, long0 = 3 * quarter, 4 * quarter
    in_col = either_in_long(first_case, bound, (quarter, 1), 0, group) > 0.5
    in_row = either_in_long(first_case, bound, (1, quarter), 1, group) > 0.5
    col_long, col_short = jnp.where(in_col, 0.0, NEG), jnp.where(in_col, NEG, 0.0)
    row_long, row_short = jnp.where(in_row, 0.0, NEG), jnp.where(in_row, NEG, 0.0)
    lane = lax.broadcasted_iota(jnp.int32, (8, 128), 1) // HEAD_DIM
    ones = (lane == lax.broadcasted_iota(jnp.int32, (8, 128), 0)).astype(F32).astype(BF16)
    sums_q, sums_v = [None] * HEADS, [None] * HEADS
    dq_copies = []

    def head_grads(j):
        for copy in dq_copies[j]:
            copy.wait()
        total = dn_s[...] if j else 0.0
        for pair in range(n_head // 2):
            packs = []
            for d in (2 * pair, 2 * pair + 1):
                i = d * local + j
                vk = ret[i, 0:rows]
                dq = lanes_to_halves(ret[i, rows : rows + rows // 2])
                dk, dv = vk[:, HEAD_DIM:], vk[:, :HEAD_DIM]
                sums_q[i] = jnp.sum(dq.astype(F32), axis=0, keepdims=True)
                sums_v[i] = jnp.sum(dv.astype(F32), axis=0, keepdims=True)
                odd = i % 2
                base = 3 * HEAD_DIM * i - HEAD_DIM * odd
                none = jnp.zeros_like(dq)
                wide = jnp.concatenate([none, dq, dk, dv] if odd else [dq, dk, dv, none], axis=1)
                total = total + dot_nt(wide, wqkv[:, base : base + 4 * HEAD_DIM])
                packs += [dq, dk, dv]
            grad = dot(normt[...], jnp.concatenate(packs, axis=1))
            if j == 0:
                put_blocks(ja, (pair, 1), grad)
            else:
                put_blocks(jb, (pair, j - 1), grad)
        dn_s[...] = total

    for j in range(local):
        for copy in do_copies[j]:
            copy.wait()
        if j + 1 < local:
            start(do_copies[j + 1])
        if j == 0:
            loads[0].wait()
            tick(*plan.get((0, "first"), ()))
        rowd = []
        for s in range(n_head):
            prod = dor[j, s].astype(F32) * own[j, s].astype(F32)
            hi = prod.astype(BF16)
            d8 = dot_nt(ones, hi) + dot_nt(ones, (prod - hi.astype(F32)).astype(BF16))
            rowd.append(jnp.concatenate([d8[0:1], d8[1:2]], axis=1))
        end = lax.select(first_case, rowd[0], rowd[3])
        full = lax.select(first_case, rowd[3], rowd[0])
        ends = [end[:, quarter * k : quarter * (k + 1)] for k in range(4)]
        first, last = lax.select(first_case, ends[0], ends[3]), lax.select(first_case, ends[3], ends[0])
        di_s[0:1, :] = jnp.concatenate([first, ends[1], ends[2], last, full, rowd[1], rowd[2]], axis=1)
        qk = sorted_blocks(first_case, [grp[j, s, 0:rows] for s in range(n_head)])
        vv = sorted_blocks(first_case, [lanes_to_halves(grp[j, s, rows : rows + rows // 2]) for s in range(n_head)])
        dd = sorted_blocks(first_case, [lanes_to_halves(dor[j, s]) for s in range(n_head)])
        at = 0
        for a, b, d in zip(qk, vv, dd):
            n = a.shape[0]
            q = a[:, :HEAD_DIM] * BF16(HEAD_DIM**-0.5)
            k_s[at : at + n] = a[:, HEAD_DIM:]
            v_s[at : at + n] = b
            qt_s[:, at : at + n] = jnp.transpose(q)
            dot_s[:, at : at + n] = jnp.transpose(d)
            block, inner = at // rows, at % rows
            dzq_s[block, inner : inner + n] = jnp.concatenate([d, jnp.zeros_like(d)], axis=1)
            dzq_s[block, rows + inner : rows + inner + n] = jnp.concatenate([jnp.zeros_like(q), q], axis=1)
            at += n
        kt_s[...] = jnp.transpose(k_s[...])
        dqt_s[...] = jnp.zeros_like(dqt_s)
        dkv_s[...] = jnp.zeros_like(dkv_s)

        def area(q0, count, k0, k1, masks):
            lanes, number = slice(q0, q0 + count), k1 - k0
            s_s[:number, :count] = dot(k_s[k0:k1], qt_s[:, lanes])
            dp_s[:number, :count] = dot(v_s[k0:k1], dot_s[:, lanes])
            for k, mask in masks.items():
                if k0 <= k < k1:
                    s_s[k - k0 : k - k0 + quarter, :count] += mask
            for at in range(0, count, LANES):
                wide = min(LANES, count - at)
                here, place = slice(at, at + wide), slice(q0 + at, q0 + at + wide)
                lse_row, di_row = lse[j : j + 1, place], di_s[0:1, place]
                for k in range(0, number, KEYS):
                    keys = slice(k, k + KEYS)
                    p = jnp.exp(s_s[keys, here] - lse_row)
                    ds = p * (dp_s[keys, here] - di_row)
                    pds_s[keys, here] = p.astype(BF16)
                    pds_s[keys, rows + at : rows + at + wide] = ds.astype(BF16)
            block, inner = q0 // rows, q0 % rows
            if count == rows:
                add = dot(pds_s[:number], dzq_s[block])
            else:
                add = dot(pds_s[:number, :count], dzq_s[block, inner : inner + count])
                add = add + dot(pds_s[:number, rows : rows + count], dzq_s[block, rows + inner : rows + inner + count])
            dkv_s[k0:k1] += add
            dqt_s[:, lanes] += dot(kt_s[:, k0:k1], pds_s[:number, rows : rows + count])

        area(0, short, 0, long0, {short: col_short})
        either = {k: row_short for k in range(0, short, quarter)}
        either[short] = jnp.where(in_row, col_long, col_short)
        either.update({k: row_long for k in range(long0, group, quarter)})
        for k in range(0, group, rows):
            area(short, quarter, k, k + rows, either)
        tick(*plan.get((j, "near"), ()))
        half_keys = (group - short) // 2
        for t in range(n_head - 1):
            for half in range(2):
                k = short + half * half_keys
                area(long0 + t * rows, rows, k, k + half_keys, {short: col_long})
                tick(*plan.get((j, 2 * t + half), ()))
        dq_s[...] = jnp.transpose(dqt_s[...] * HEAD_DIM**-0.5).astype(BF16)

        dkv = unsorted_blocks(first_case, dkv_s[...])
        dqu = unsorted_blocks(first_case, dq_s[...])
        for s in range(n_head):
            msg[j, s, 0:rows] = dkv[s].astype(BF16)
            msg[j, s, rows : rows + rows // 2] = halves_to_lanes(dqu[s])
        dq_copies.append(spread(j, lambda d, j=j: msg.at[j, d], lambda s, j=j: ret.at[s * local + j], dq_send, dq_recv))
        start(dq_copies[j])
        if j == 0:
            for load in loads[1:]:
                load.wait()
            normt[...] = jnp.transpose(sent_s[...])
        else:
            head_grads(j - 1)
        tick(*plan.get((j, "end"), ()))

    head_grads(local - 1)
    tick(*plan.get("last", ()))
    share = as_column(as_line(mixw_r))
    gain = as_line(gain_r).astype(F32)
    sums = [jnp.zeros((1, width), F32)] * 2
    scaled = []
    step = 128
    for r in range(0, rows, step):
        part = slice(r, r + step)
        mix = mixed[part]
        mean = jnp.mean(mix, axis=1, keepdims=True)
        centered = mix - mean
        rstd = lax.rsqrt(jnp.mean(centered * centered, axis=1, keepdims=True) + EPS)
        unit = centered * rstd
        dn = dn_s[part]
        e = dn * gain
        inner = e - jnp.mean(e, axis=1, keepdims=True) - unit * jnp.mean(e * unit, axis=1, keepdims=True)
        grad = mg_s[part] + rstd * inner
        sums[0] = sums[0] + jnp.sum(dn * unit, axis=0, keepdims=True)
        sums[1] = sums[1] + jnp.sum(dn, axis=0, keepdims=True)
        mixed[part] = share[part] * grad
        dn_s[part] = (1.0 - share[part]) * grad
    chosen = lax.broadcasted_iota(jnp.int32, (rows, rows), 0) == as_line(prow_r)
    chosen = chosen.astype(F32).astype(BF16)
    given = dn_s[...]
    high = given.astype(BF16)
    low = (given - high.astype(F32)).astype(BF16)
    sent_s[...] = (dot(chosen, high) + dot(chosen, low)).astype(BF16)
    far_copy = pltpu.make_async_remote_copy(
        src_ref=sent_s, dst_ref=back_s, send_sem=far_sem.at[0], recv_sem=far_sem.at[1], device_id=(far, h), device_id_type=MESH
    )
    far_copy.start()
    sm_o[...] = sm_in[...]
    sm_o[0:1, :] = sums[0]
    sm_o[1:2, :] = sums[1]
    sm_o[2:3, :] = jnp.concatenate(sums_q, axis=1)
    sm_o[3:4, :] = jnp.concatenate(sums_v, axis=1)
    if cut:
        def small_sum():
            for k, axis in enumerate(("core", "x", "y", "lo", "hi")):
                copy = pltpu.make_async_remote_copy(
                    src_ref=sm_o, dst_ref=sm_r.at[k], send_sem=sm_send.at[k], recv_sem=sm_recv.at[k],
                    device_id=near[axis], device_id_type=MESH,
                )
                copy.start()
                yield
                copy.wait()
                sm_o[...] += sm_r[k]

        small = small_sum()
        tick(small, jobb, fc3, fc4, joba, fc1, fc2, small, fc3, fc4, joba, small, fc3, joba, jobb, small, jobb, small, jobb)
    else:
        fin_o[0] = ja[...]
        fin_o[1] = jb[...]
    far_copy.wait()
    for r in range(0, rows, step):
        part = slice(r, r + step)
        grad_o[part] = (mixed[part] + back_s[part].astype(F32)).astype(BF16)
    if cut:
        tick(small, joba, jobb, joba, jobb)


def back(n_crop, n_head, cut, attg, grp, own, lse, jfc, gout, wqkv, normed, mixed, mg, mixw, prow, crop, gain, sm):
    rows, width = mixed.shape
    group, local = rows * n_head, HEADS // n_head
    vmem = pl.BlockSpec(memory_space=pltpu.VMEM)
    hbm = pl.BlockSpec(memory_space=pl.ANY)
    smem = pl.BlockSpec(memory_space=pltpu.SMEM)
    dma = pltpu.SemaphoreType.DMA
    shape = jax.ShapeDtypeStruct
    block = rows + rows // 2
    jq_dims = (2, 2, 2, 2, 2, 96, PIECE) if cut else (2, 2, width, PIECE)
    finals = (6, 2, 2, 96, PIECE) if cut else (2, *jq_dims)
    square = lambda n, kind: pltpu.VMEM((group, n), kind)
    scratch = [
        pltpu.VMEM((local, n_head, block, 128), BF16),
        pltpu.VMEM(wqkv.shape, BF16),
        pltpu.VMEM((width, rows), BF16),
        pltpu.VMEM((rows, width), F32),
        pltpu.VMEM((rows, width), F32),
        pltpu.VMEM((local, n_head, rows // 2, 128), BF16),
        square(HEAD_DIM, BF16), square(HEAD_DIM, BF16),
        pltpu.VMEM((HEAD_DIM, group), BF16), pltpu.VMEM((HEAD_DIM, group), BF16), pltpu.VMEM((HEAD_DIM, group), BF16),
        pltpu.VMEM((HEAD_DIM, group), F32),
        pltpu.VMEM((832, rows), F32), pltpu.VMEM((832, rows), F32), pltpu.VMEM((832, 2 * rows), BF16),
        pltpu.VMEM((n_head, 2 * rows, 128), BF16), square(128, F32), square(HEAD_DIM, BF16),
        pltpu.VMEM((8, group), F32),
        pltpu.VMEM((local, n_head, block, 128), BF16),
        pltpu.VMEM((HEADS, block, 128), BF16),
        pltpu.VMEM((rows, width), F32),
        pltpu.VMEM((rows, width), BF16),
        pltpu.VMEM((rows, width), BF16),
        pltpu.VMEM(jq_dims, BF16),
        pltpu.VMEM(jq_dims, BF16),
        dma((7,)),
        dma((local, n_head - 1)), dma((local, n_head - 1)), dma((local, n_head - 1)), dma((local, n_head - 1)),
        dma((local,)),
        dma((2,)),
    ]
    if cut:
        scratch += [dma((6, 9)), dma((6, 9)), dma((4,)), dma((5,)), dma((5,)), pltpu.VMEM((5, 16, width), F32)]
        scratch.append(pltpu.VMEM((4, 2, 2, 2, 2, 96, PIECE), BF16))
        scratch += [pltpu.VMEM((6,) + (2,) * n + (96, PIECE), BF16) for n in (4, 3, 2, 1, 0)]
    return pl.pallas_call(
        functools.partial(back_kernel, n_crop, n_head, cut),
        out_shape=(shape((rows, width), BF16), shape(finals, BF16), shape((16, width), F32)),
        in_specs=[hbm, hbm, vmem, vmem, hbm, hbm, hbm, hbm, hbm, hbm, vmem, vmem, smem, vmem, vmem],
        out_specs=(vmem,) * 3,
        scratch_shapes=scratch,
        compiler_params=pltpu.CompilerParams(collective_id=2, has_side_effects=True, vmem_limit_bytes=60 * MiB),
        cost_estimate=pl.CostEstimate(flops=2 * 10**10, bytes_accessed=3 * 10**7, transcendentals=10**7),
        name="back",
    )(attg, grp, own, lse, jfc, gout, wqkv, normed, mixed, mg, mixw, prow, crop, gain, sm)


def finish_kernel(n_crop, n_head, grad, fin, sm, *outs):
    grad_o, g1_o, b1_o, gq_o, bq_o, bv_o, go_o, bo_o, g2_o, b2_o, gf1_o, bf1_o, gf2_o, bf2_o = outs
    c = lax.axis_index("crop")
    local = HEADS // n_head
    grad_o[...] = grad[...]
    parts = []
    for k in range(4):
        core, x = k % 2, k // 2
        for half in range(2):
            at = FC_TILE * k + PIECE * half
            gf1_o[:, at : at + PIECE] = fin[half, core, x].astype(F32)
        both = jnp.concatenate([fin[2, core, x], fin[3, core, x]], axis=0)
        parts.append(jnp.transpose(both.astype(F32)))
    gf2_o[...] = jnp.concatenate(parts, axis=1)
    for k in range(2):
        go_o[:, PIECE * k : PIECE * (k + 1)] = fin[4, k, 0].astype(F32)
    parts = []
    for i in range(HEADS):
        d, j = i // local, i % local
        piece = fin[4, d // 2, 1] if j == 0 else fin[5, d // 2, j - 1]
        parts.append(piece[:, 192 * (d % 2) : 192 * (d % 2 + 1)].astype(F32))
    gq_o[...] = jnp.concatenate(parts, axis=1)
    piece = jnp.zeros((16, 96), F32)
    wide = jnp.zeros((1, PIECE), F32)
    for k in range(n_crop):
        piece = lax.select(c == k, sm[:, 96 * k : 96 * (k + 1)], piece)
        wide = lax.select(c == k, sm[8 + k // 2 : 9 + k // 2, PIECE * (k % 2) : PIECE * (k % 2 + 1)], wide)
    for row, out in ((0, g1_o), (1, b1_o), (2, bq_o), (3, bv_o), (4, bo_o), (5, g2_o), (6, b2_o), (7, bf2_o)):
        out[...] = piece[row : row + 1].reshape(96)
    bf1_o[...] = wide.reshape(PIECE)


def finish(n_crop, n_head, grad, fin, sm):
    rows, width = grad.shape
    vmem = pl.BlockSpec(memory_space=pltpu.VMEM)
    shape = jax.ShapeDtypeStruct
    short = shape((96,), F32)
    outs = (
        shape((rows, width), BF16), short, short, shape((96, 3 * width), F32), short, short, shape((96, width), F32), short,
        short, short, shape((96, 4 * width), F32), shape((PIECE,), F32), shape((PIECE, width), F32), short,
    )
    return pl.pallas_call(
        functools.partial(finish_kernel, n_crop, n_head),
        out_shape=outs,
        in_specs=[vmem] * 3,
        out_specs=(vmem,) * len(outs),
        compiler_params=pltpu.CompilerParams(vmem_limit_bytes=60 * MiB),
        name="finish",
    )(grad, fin, sm)


def sum_everywhere(grads, small, n_crop, n_head):
    c = lax.axis_index("crop")

    def scatter(value):
        part = lax.psum_scatter(value.astype(F32), "crop", scatter_dimension=0, tiled=True)
        return lax.psum(part.astype(BF16), "head").astype(F32)

    jfc, ja, jb = grads
    width = jfc.shape[3]
    local = HEADS // n_head
    g1 = jnp.concatenate([jfc[half, t % 2, t // 2] for t in range(4) for half in range(2)], axis=1)
    g2 = jnp.concatenate([jfc[2 + half, t % 2, t // 2] for t in range(4) for half in range(2)], axis=1).T
    go = jnp.concatenate([ja[0, 0], ja[1, 0]], axis=1)
    parts = []
    for i in range(HEADS):
        d, j = i // local, i % local
        piece = ja[d // 2, 1] if j == 0 else jb[d // 2, j - 1]
        parts.append(piece[:, 192 * (d % 2) : 192 * (d % 2 + 1)])
    gq = jnp.concatenate(parts, axis=1)
    total = lax.psum(small, ("crop", "head"))

    def mine(vector):
        count = vector.shape[0] // n_crop
        return lax.dynamic_slice_in_dim(vector, c * count, count, 0)

    rows = [mine(total[k]) for k in range(8)]
    return [
        rows[0], rows[1], scatter(gq), rows[2], rows[3], scatter(go), rows[4], rows[5], rows[6],
        scatter(g1), mine(total[8:12].reshape(4 * width)), scatter(g2), rows[7],
    ]


def shards(
    tokens, mix_weight, partner_row, crop_lengths, ln1_gain, ln1_bias, w_qkv, b_query, b_value, w_out, b_out,
    ln2_gain, ln2_bias, w_fc1, b_fc1, w_fc2, b_fc2, cotangent,
):
    n_crop, n_head = lax.axis_size("crop"), lax.axis_size("head")
    cut = n_crop == 8 and n_head == 4
    small1, small2 = (ln1_gain, ln1_bias, b_query, b_value), (b_out, ln2_gain, ln2_bias, b_fc2, b_fc1)
    mixed, normed, grp, att, own, lse, gw, cott, gsum = front(
        n_crop, n_head, tokens, mix_weight, partner_row, crop_lengths, small1, w_qkv, cotangent, w_fc2
    )
    layer_out, attg, mg, jfc, gout, sm = middle(cut, att, mixed, cotangent, cott, gsum, small2, w_out, w_fc1, w_fc2, gw)
    grad, fin, sm = back(
        n_crop, n_head, cut, attg, grp, own, lse, jfc, gout, w_qkv, normed, mixed, mg, mix_weight, partner_row, crop_lengths, ln1_gain, sm
    )
    if not cut:
        return (layer_out, grad, *sum_everywhere((jfc, fin[0], fin[1]), sm, n_crop, n_head))
    outs = finish(n_crop, n_head, grad, fin, sm)
    return (layer_out, *outs)


def solution(mesh):
    rows, one = P(("crop", "head"), None), P(("crop", "head"))
    in_specs = (rows, one, one, P("crop", None)) + (P(),) * 13 + (rows,)
    vector, matrix = P("crop"), P("crop", None)
    out_specs = (
        rows, rows, vector, vector, matrix, vector, vector, matrix, vector, vector, vector, matrix, vector, matrix, vector,
    )
    return jax.shard_map(shards, mesh=mesh, in_specs=in_specs, out_specs=out_specs, check_vma=False)
```

profile of v0, /device:TPU:1, one launch (start us, length us, event | category | flops | bytes accessed | tf_op | source)
XLA Modules:
  0.0 256.5 jit_solution(17523675445193770349)
XLA Ops:
  0.6 86.0 %front.1 = (f32[512,768]{1,0:T(8,128)}, bf16[512,768]{1,0:T(8,128)(2,1)}, bf16[3,4,768,128]{3,2,1,0:T(8,128)(2,1)}, bf16[512,768]{1,0:T(8,128)(2,1)}, bf16[3,4,2...) custom-call(bf16[512,768]{1,0:T(8,128)(2,1)} %tokens.1, ...), custom_call_target="tpu_custom_call" | custom-call | flops 10000000000 | bytes 20000000 | tf_op jit(solution)/shard_map/front/pallas_call | solution.py:286
  86.7 26.5 %middle.1 = (bf16[512,768]{1,0:T(8,128)(2,1)}, bf16[12,256,128]{2,1,0:T(8,128)(2,1)}, f32[512,768]{1,0:T(8,128)}, bf16[4,2,2,2,2,2,96,384]{7,6,5,4,3,2,1,0:T(8,1...) custom-call(bf16[512,768]{1,0:T(8,128)(2,1)} %get-tuple-element.47.att, ...), custom_call_target="tpu_custom_call" | custom-call | flops 16000000000 | bytes 30000000 | tf_op jit(solution)/shard_map/middle/pallas_call | solution.py:484
  113.2 138.4 %back.1 = (bf16[512,768]{1,0:T(8,128)(2,1)}, bf16[6,2,2,96,384]{4,3,2,1,0:T(8,128)(2,1)}, f32[16,768]{1,0:T(8,128)}) custom-call(bf16[12,256,128]{2,1,0:T(8,128)(2,1)} %get-tuple-element.53.attg, bf16[3,4,768,128]{3,2,1,0:T(8,128)(2,1)} %get-tuple-element.54.grp_h, bf16[3,4,256,128]{3,2,1,0:T(8,128)(2,1)} %get-tuple-element.55.own, ...), custom_call_target="tpu_custom_call" | custom-call | flops 20000000000 | bytes 30000000 | tf_op jit(solution)/shard_map/back/pallas_call | solution.py:894
  251.6 4.6 %finish.1 = (bf16[512,768]{1,0:T(8,128)(2,1)}, f32[96]{0:T(128)}, f32[96]{0:T(128)}, f32[96,2304]{1,0:T(8,128)}, f32[96]{0:T(128)}, /*index=5*/f32[96]{0:T(128)}...) custom-call(bf16[512,768]{1,0:T(8,128)(2,1)} %get-tuple-element.62.g, ...), custom_call_target="tpu_custom_call" | custom-call | tf_op jit(solution)/shard_map/finish/pallas_call | solution.py:947
where the time goes:
time: 261 us; the launch traced here: 256 us
  Pallas kernels  256 us (98%)
    pallas_call x1, Pallas kernels, back(): pl.pallas_call(functools.partial(back_kernel, n_crop, n_head, cut), out_s...  138 us
    pallas_call x1, Pallas kernels, front(): pl.pallas_call(functools.partial(front_kernel, n_crop, n_head), out_shape...  86 us
    pallas_call x1, Pallas kernels, middle(): pl.pallas_call(functools.partial(middle_kernel, cut), out_shape=(shape((r...  26.5 us

commit v1 on v0

--- a/solution.py
+++ b/solution.py
@@ -177,10 +177,9 @@
                     device_id_type=MESH,
                 )
             )
+        for copy in batch:
+            copy.start()
         qkv_copies.append(batch)
-        if j == 0:
-            for copy in batch:
-                copy.start()
 
     bound = crop[0, 0]
     first_case = bound < group // 2
@@ -194,9 +193,6 @@
     for j in range(local):
         for copy in qkv_copies[j]:
             copy.wait()
-        if j + 1 < local:
-            for copy in qkv_copies[j + 1]:
-                copy.start()
         qk = sorted_blocks(first_case, [grp[j, s, 0:rows] for s in range(n_head)])
         vv = sorted_blocks(first_case, [lanes_to_halves(grp[j, s, rows : rows + rows // 2]) for s in range(n_head)])
         at = 0
@@ -554,9 +550,7 @@
             copy.wait()
             self.add(self.acc, self.received[1 + k], lead, free)
         bc, bx = self.bits["core"], self.bits["x"]
-        mine = pltpu.make_async_copy(self.acc.at[tuple(lead)], self.fin.at[bc, bx], self.send_sem.at[8])
-        mine.start()
-        mine.wait()
+        self.fin[bc, bx] = self.acc[tuple(lead)]
         copies = [
             self.remote(5 + n, self.fin.at[bc, bx], self.fin.at[bc, bx], None, other) for n, other in enumerate(self.others)
         ]

time: 261 us -> 257 us (0.985)
  Pallas kernels: 256 us -> 252 us
    pallas_call x1, Pallas kernels: 86 us -> 82.9 us  [front(): pl.pallas_call(functools.partial(front_kernel, n_crop, n_head), out_shape...]
where the time goes in v1:
time: 257 us; the launch traced here: 253 us
  Pallas kernels  252 us (98%)
    pallas_call x1, Pallas kernels, back(): pl.pallas_call(functools.partial(back_kernel, n_crop, n_head, cut), out_s...  138 us
    pallas_call x1, Pallas kernels, front(): pl.pallas_call(functools.partial(front_kernel, n_crop, n_head), out_shape...  82.9 us
    pallas_call x1, Pallas kernels, middle(): pl.pallas_call(functools.partial(middle_kernel, cut), out_shape=(shape((r...  26.5 us

profile of v1, /device:TPU:1, one launch (start us, length us, event | category | flops | bytes accessed | tf_op | source)
XLA Modules:
  0.0 252.9 jit_solution(4066458026817003515)
XLA Ops:
  0.6 82.9 %front.1 = (f32[512,768]{1,0:T(8,128)}, bf16[512,768]{1,0:T(8,128)(2,1)}, bf16[3,4,768,128]{3,2,1,0:T(8,128)(2,1)}, bf16[512,768]{1,0:T(8,128)(2,1)}, bf16[3,4,2...) custom-call(bf16[512,768]{1,0:T(8,128)(2,1)} %tokens.1, ...), custom_call_target="tpu_custom_call" | custom-call | flops 10000000000 | bytes 20000000 | tf_op jit(solution)/shard_map/front/pallas_call | solution.py:282
  83.5 26.5 %middle.1 = (bf16[512,768]{1,0:T(8,128)(2,1)}, bf16[12,256,128]{2,1,0:T(8,128)(2,1)}, f32[512,768]{1,0:T(8,128)}, bf16[4,2,2,2,2,2,96,384]{7,6,5,4,3,2,1,0:T(8,1...) custom-call(bf16[512,768]{1,0:T(8,128)(2,1)} %get-tuple-element.47.att, ...), custom_call_target="tpu_custom_call" | custom-call | flops 16000000000 | bytes 30000000 | tf_op jit(solution)/shard_map/middle/pallas_call | solution.py:480
  110.1 138.0 %back.1 = (bf16[512,768]{1,0:T(8,128)(2,1)}, bf16[6,2,2,96,384]{4,3,2,1,0:T(8,128)(2,1)}, f32[16,768]{1,0:T(8,128)}) custom-call(bf16[12,256,128]{2,1,0:T(8,128)(2,1)} %get-tuple-element.53.attg, bf16[3,4,768,128]{3,2,1,0:T(8,128)(2,1)} %get-tuple-element.54.grp_h, bf16[3,4,256,128]{3,2,1,0:T(8,128)(2,1)} %get-tuple-element.55.own, ...), custom_call_target="tpu_custom_call" | custom-call | flops 20000000000 | bytes 30000000 | tf_op jit(solution)/shard_map/back/pallas_call | solution.py:888
  248.0 4.6 %finish.1 = (bf16[512,768]{1,0:T(8,128)(2,1)}, f32[96]{0:T(128)}, f32[96]{0:T(128)}, f32[96,2304]{1,0:T(8,128)}, f32[96]{0:T(128)}, /*index=5*/f32[96]{0:T(128)}...) custom-call(bf16[512,768]{1,0:T(8,128)(2,1)} %get-tuple-element.62.g, ...), custom_call_target="tpu_custom_call" | custom-call | tf_op jit(solution)/shard_map/finish/pallas_call | solution.py:941
